TPU v7x, 128 devices: a whole 4x4x4 slice. The times are simulated.
128 devices in a mesh: row: 16 (over x, z_hi, core), col: 8 (over y, z_lo).
Axes of the slice: x: 4, y: 4, z: 4 (z_hi: 2, z_lo: 2; z = z_hi * 2 + z_lo), core: 2. Of those that a mesh axis runs over, the one named last changes fastest.
Arguments:
- tokens: bfloat16 [2, 256, 384, 512], P(None, 'row', 'col'), may hold values from -8 to 8
- region: int32 [256, 384], P('row', 'col'), may hold values from 0 to 2, as said below
- w_qkv: bfloat16 [512, 1536], P(('row', 'col')), may hold values from -0.25 to 0.25
- w_proj: bfloat16 [512, 512], P(('row', 'col')), may hold values from -0.25 to 0.25
- w_fc1: bfloat16 [512, 2048], P(('row', 'col')), may hold values from -0.25 to 0.25
- w_fc2: bfloat16 [2048, 512], P(('row', 'col')), may hold values from -0.125 to 0.125
- gain_attn: float32 [512], replicated, may hold values from 0.5 to 1.5
- gain_mlp: float32 [512], replicated, may hold values from 0.5 to 1.5
- table: float32 [961, 16], replicated, may hold values from -4 to 4
- index: int32 [256, 256], replicated, may hold values from 0 to 960
- logit_scale: float32 [16], replicated, may hold values from 3 to 10
Outputs:
- block_out: bfloat16 [2, 256, 384, 512], P(None, 'row', 'col')
Inputs may be any that keep to these rules, and one draw needn't show every extreme that they name: The shifted grid falls into nine regions: rows before 256 - 16, rows from there before 256 - 8, and the last 8 rows, crossed with the same three parts of the columns; all positions of one region share a label, and each label is that of exactly three regions.
All inputs are finite; a program needn't handle non-finite values.
Results may differ from a plain program's by a relative error of at most 0.02.
Values may be sent and summed in bfloat16 or wider, within the bound.
A program may use at most 128 MiB of HBM per device.

v0:
```python
import jax
import jax.numpy as jnp
from jax import lax
from jax.sharding import PartitionSpec as P

HEADS = 16
WINDOW = 16
SHIFT = 8


def from_behind(block, axis, distance):
    devices = range(lax.axis_size(axis))
    route = [((i - distance) % len(devices), i) for i in devices]
    return lax.ppermute(block, axis, route)


def unit_length(vectors):
    return vectors / jnp.maximum(jnp.sqrt(jnp.sum(vectors * vectors, -1, keepdims=True)), 1.0)


def normed(value, gain):
    mean_val = jnp.mean(value, -1, keepdims=True)
    centered = value - mean_val
    variance = jnp.mean(centered * centered, -1, keepdims=True)
    return centered * lax.rsqrt(variance + 1e-05) * gain


def position_bias(table, index):
    return jnp.transpose(16.0 * jax.nn.sigmoid(table[index]), (2, 0, 1))


def windowed(tile_in, labels_tile, side):
    images, tile_rows, tile_cols, channels = tile_in.shape
    blocks = tile_in.reshape(images, tile_rows // side, side, tile_cols // side, side, channels)
    blocks = blocks.transpose(0, 1, 3, 2, 4, 5).reshape(-1, side * side, channels)
    labels = labels_tile.reshape(tile_rows // side, side, tile_cols // side, side)
    labels = labels.transpose(0, 2, 1, 3).reshape(-1, side * side)
    return (blocks, jnp.tile(labels, (images, 1)))


def unwindow(blocks, images, tile_rows, tile_cols, side):
    channels = blocks.shape[-1]
    grid = blocks.reshape(images, tile_rows // side, tile_cols // side, side, side, channels)
    return grid.transpose(0, 1, 3, 2, 4, 5).reshape(images, tile_rows, tile_cols, channels)


def attention(blocks, labels, w_qkv, w_proj, pos_bias, logit_scale):
    num_windows, win_length, channels = blocks.shape
    projected = jnp.dot(
        blocks.reshape(num_windows * win_length, channels),
        w_qkv,
        preferred_element_type=jnp.float32,
    ).astype(jnp.bfloat16)
    projected = projected.reshape(num_windows, win_length, 3, HEADS, channels // HEADS)
    queries = unit_length(projected[:, :, 0].astype(jnp.float32))
    key_unit = unit_length(projected[:, :, 1].astype(jnp.float32))
    values = projected[:, :, 2]
    cosine = jnp.einsum("wqhd,wkhd->whqk", queries, key_unit)
    same_region = labels[:, :, None] == labels[:, None, :]
    mask_add = jnp.where(same_region, 0.0, -100.0).astype(jnp.float32)
    scores = cosine * logit_scale[None, :, None, None] + pos_bias[None] + mask_add[:, None]
    exponent = jnp.exp(scores)
    weights = (exponent / jnp.sum(exponent, -1, keepdims=True)).astype(jnp.bfloat16)
    mixed_heads = jnp.einsum(
        "whqk,wkhd->wqhd", weights, values, preferred_element_type=jnp.float32
    ).astype(jnp.bfloat16)
    mixed_heads = mixed_heads.reshape(num_windows * win_length, channels)
    return (
        jnp.dot(mixed_heads, w_proj, preferred_element_type=jnp.float32)
        .astype(jnp.bfloat16)
        .reshape(num_windows, win_length, channels)
    )


def finish_block(tokens_flat, attended, w_fc1, w_fc2, gain_attn, gain_mlp):
    after_attn = (
        tokens_flat.astype(jnp.float32) + normed(attended.astype(jnp.float32), gain_attn)
    ).astype(jnp.bfloat16)
    hidden = jax.nn.gelu(
        jnp.dot(after_attn, w_fc1, preferred_element_type=jnp.float32), approximate=False
    ).astype(jnp.bfloat16)
    mlp_out = jnp.dot(hidden, w_fc2, preferred_element_type=jnp.float32)
    return (after_attn.astype(jnp.float32) + normed(mlp_out, gain_mlp)).astype(jnp.bfloat16)


def body(
    tokens, region, w_qkv, w_proj, w_fc1, w_fc2, gain_attn, gain_mlp, table, index, logit_scale
):
    full_qkv, full_proj, full_fc1, full_fc2 = (
        lax.all_gather(w_qkv, ("row", "col"), axis=0, tiled=True),
        lax.all_gather(w_proj, ("row", "col"), axis=0, tiled=True),
        lax.all_gather(w_fc1, ("row", "col"), axis=0, tiled=True),
        lax.all_gather(w_fc2, ("row", "col"), axis=0, tiled=True),
    )
    images, tile_rows, tile_cols, channels = tokens.shape
    pos_bias = position_bias(table, index)
    row_piece = from_behind(tokens[:, :SHIFT], "row", -1)
    rows_rolled = jnp.concatenate([tokens[:, SHIFT:], row_piece], 1)
    side_strip = from_behind(rows_rolled[:, :, :SHIFT], "col", -1)
    rolled = jnp.concatenate([rows_rolled[:, :, SHIFT:], side_strip], 2)
    blocks, labels = windowed(rolled, region, WINDOW)
    mixed_out = attention(blocks, labels, full_qkv, full_proj, pos_bias, logit_scale)
    attended = unwindow(mixed_out, rolled.shape[0], rolled.shape[1], rolled.shape[2], WINDOW)
    total = images * tile_rows * tile_cols
    returned = from_behind(attended[:, :, tile_cols - SHIFT :], "col", 1)
    col_done = jnp.concatenate([returned, attended[:, :, : tile_cols - SHIFT]], 2)
    row_back = from_behind(col_done[:, tile_rows - SHIFT :], "row", 1)
    restored = jnp.concatenate([row_back, col_done[:, : tile_rows - SHIFT]], 1)
    block_out = finish_block(
        tokens.reshape(total, channels),
        restored.reshape(total, channels),
        full_fc1,
        full_fc2,
        gain_attn,
        gain_mlp,
    )
    return block_out.reshape(images, tile_rows, tile_cols, channels)


def solution(mesh):
    return jax.shard_map(
        body,
        mesh=mesh,
        in_specs=(
            P(None, "row", "col", None),
            P("row", "col"),
            P(("row", "col"), None),
            P(("row", "col"), None),
            P(("row", "col"), None),
            P(("row", "col"), None),
            P(),
            P(),
            P(),
            P(),
            P(),
        ),
        out_specs=P(None, "row", "col", None),
        check_vma=False,
    )
```

profile of v0, /device:TPU:1, one launch (start us, length us, event | category | flops | bytes accessed | tf_op | source)
XLA Modules:
  0.0 957.8 jit_solution(6531080252570511876)
XLA Ops:
  9.5 1.5 collective-permute-start
  11.5 215.9 %gather_fusion = f32[65536,16]{1,0:T(8,128)} fusion(f32[961,16]{1,0:T(8,128)S(1)} %copy.55, s32[65536]{0:T(1024)S(1)} %broadcast_clamp_fusion), kind=kCustom, calls=%fused_computation | custom fusion | bytes 8650752 | tf_op jit(solution)/shard_map/gather | solution.py:29
  227.4 19.1 %copy.56 = f32[65536,16]{0,1:T(8,128)} copy(f32[65536,16]{1,0:T(8,128)} %gather_fusion) | data formatting | bytes 8388608 | tf_op jit(solution)/shard_map/gather | solution.py:29
  246.5 5.4 divide_multiply_fusion
  253.5 4.2 collective-permute-start.1
  257.7 301.1 %all-gather.1 = bf16[128,4,512]{2,1,0:T(4,128)(2,1)S(1)} all-gather(bf16[1,4,512]{2,1,0:T(4,128)(2,1)S(1)} %bitcast.83), channel_id=1, replica_groups=mesh['row'=16,'col'=8] {'row','col'}, dimensions={0}, use_global_device_ids=true | all-gather | bytes 528384 | tf_op jit(solution)/shard_map/all_gather | solution.py:91
  558.9 5.4 copy.65
  564.2 5.8 copy.57
  571.5 2.7 reshape.125
  574.2 4.3 convolution_convert_fusion
  578.5 6.6 copy.51
  585.1 10.3 %reshape.101 = bf16[6,256,3,16,32]{1,0,4,3,2:T(8,128)(2,1)} reshape(bf16[1536,1536]{0,1:T(8,128)(2,1)} %copy.51) | data formatting | bytes 9437184 | tf_op jit(solution)/shard_map/reshape | solution.py:54
  595.4 3.5 fusion.14
  599.5 3.2 convert_divide_fusion.1
  602.7 15.9 %fusion = (f32[6,16,256]{2,1,0:T(8,128)S(1)}, f32[6,16,256,256]{2,3,1,0:T(8,128)}) fusion(f32[6,256,256]{1,2,0:T(8,128)} %compare_select_fusion, f32[16,256,256]{1,2,0:T(8,128)S(1)} %copy-done.1, f32[16]{0:T(128)S(1)} %copy-done.10, bf16[6,256,16,32]{1,0,3,2:T(8,128)(2,1)} %get-tuple-element.8, bf16[6,256,16,32]{1,0,3,2:T(8,128)(2,1)} %get-tuple-element.7), kind=kOutput, calls=%fused_computation.3 | convolution fusion | flops 427794432 | bytes 34177088 | tf_op jit(solution)/shard_map/wqhd,wkhd->whqk/dot_general | solution.py:58
  618.6 13.6 %fusion.27 = bf16[6,256,16,32]{1,3,2,0:T(8,128)(2,1)} fusion(f32[6,16,256,256]{2,3,1,0:T(8,128)} %get-tuple-element.12, f32[6,16,256]{2,1,0:T(8,128)S(1)} %get-tuple-element.11, f32[6,256,256]{1,2,0:T(8,128)} %compare_select_fusion, f32[16,256,256]{1,2,0:T(8,128)S(1)} %copy-done.2, f32[16]{0:T(128)S(1)} %copy-done.10, ...), kind=kOutput, calls=%fused_computation.59 | convolution fusion | flops 434896896 | bytes 34177088 | tf_op jit(solution)/shard_map/whqk,wkhd->wqhd/dot_general | solution.py:64
  632.2 2.6 copy.60
  637.7 6.3 collective-permute-done.2
  644.1 4.0 reshape.129
  648.1 15.4 %collective-permute-done.3 = bf16[2,8,48,512]{3,2,1,0:T(8,128)(2,1)S(1)} collective-permute-done((bf16[2,8,48,512]{3,2,1,0:T(8,128)(2,1)S(1)}, bf16[2,8,48,512]{3,2,1,0:T(8,128)(2,1)S(1)}, u32[]{:S(2)}, u32[]{:S(2)}) %collective-permute-start.3) | collective-permute-done | bytes 786464 | tf_op jit(solution)/shard_map/ppermute | solution.py:14
  666.1 1.9 fusion.18
  668.0 246.9 %all-gather.7.cloned.1.call-done = bf16[2048,512]{1,0:T(8,128)(2,1)} async-done(((bf16[16,512]{1,0:T(8,128)(2,1)}), bf16[2048,512]{1,0:T(8,128)(2,1)}) %all-gather.7.cloned.1.call-update) | async-done | bytes 2097168 | tf_op jit(solution)/shard_map/all_gather | solution.py:93
  914.9 32.9 %fusion.63 = (f32[1536]{0:T(1024)S(1)}, f32[1536,512]{1,0:T(8,128)S(1)}) fusion(bf16[2048,512]{1,0:T(8,128)(2,1)} %all-gather.7.cloned.1.call-done, bf16[1536,512]{1,0:T(8,128)(2,1)} %fusion.18, bf16[512,2048]{1,0:T(8,128)(2,1)} %reshape.129), kind=kOutput, calls=%fused_computation.104 | convolution fusion | flops 6647708160 | bytes 8919040 | tf_op jit(solution)/shard_map/dot_general | solution.py:82
  949.2 1.9 add_convert_fusion
  (73 shorter events, 13.9 us)
Async XLA Ops:
  6.5 4.5 copy-start.7
  6.5 4.7 copy-start.6
  6.5 564.9 %all-gather.9.cloned.1.call-start = ((), (), s32[]{:S(2)}) async-start(), calls=%async_computation.1 | async-start | bytes 1585152 | tf_op jit(solution)/shard_map/all_gather | solution.py:90
  7.3 636.9 %all-gather.11.cloned.1.call-start = ((), (), s32[]{:S(2)}) async-start(), calls=%async_computation.2 | async-start | bytes 2113536 | tf_op jit(solution)/shard_map/all_gather | solution.py:92
  8.0 906.9 %all-gather.7.cloned.1.call-start = ((), (), s32[]{:S(2)}) async-start(), calls=%async_computation | async-start | bytes 2113536 | tf_op jit(solution)/shard_map/all_gather | solution.py:93
  9.5 243.9 %collective-permute-start = (bf16[2,8,48,512]{3,2,1,0:T(8,128)(2,1)S(1)}, bf16[2,8,48,512]{3,2,1,0:T(8,128)(2,1)S(1)}, u32[]{:S(2)}, u32[]{:S(2)}) collective-permute-start(bf16[2,8,48,512]{3,2,1,0:T(8,128)(2,1)S(1)} %get-tuple-element.10), channel_id=1, source_target_pairs={{8,0},{16,8},{24,16},{32,24},{40,32},{48,40},{56,48},{64,56},{72,6... | collective-permute-start | bytes 2359304 | tf_op jit(solution)/shard_map/ppermute | solution.py:14
  246.5 5.4 copy-start.8
  251.9 5.9 copy-start.9
  253.5 317.6 %collective-permute-start.1 = (bf16[2,16,8,512]{3,2,1,0:T(8,128)(2,1)S(1)}, bf16[2,16,8,512]{3,2,1,0:T(8,128)(2,1)S(1)}, u32[]{:S(2)}, u32[]{:S(2)}) collective-permute-start(bf16[2,16,8,512]{3,2,1,0:T(8,128)(2,1)S(1)} %pad_maximum_fusion.2), channel_id=1, source_target_pairs={{1,0},{2,1},{3,2},{4,3},{5,4},{6,5},{7,6},{0,7},{9,8},{10,9},{11,1... | collective-permute-start | bytes 786440 | tf_op jit(solution)/shard_map/ppermute | solution.py:14
  595.4 4.1 copy-start
  599.5 3.2 copy-start.1
  599.5 3.2 copy-start.10
  602.7 15.9 %slice-start = ((bf16[6,256,3,16,32]{1,0,4,3,2:T(8,128)(2,1)}), bf16[6,256,1,16,32]{1,0,4,3,2:T(8,128)(2,1)S(1)}, s32[]{:S(2)}) async-start(bf16[6,256,3,16,32]{1,0,4,3,2:T(8,128)(2,1)} %reshape.101), calls=%async_computation.3 | async-start | bytes 4194304 | tf_op jit(solution)/shard_map/slice | solution.py:57
  602.7 15.9 %copy-start.2 = (f32[16,256,256]{1,2,0:T(8,128)S(1)}, f32[16,256,256]{1,2,0:T(8,128)}, u32[]{:S(2)}) copy-start(f32[16,256,256]{1,2,0:T(8,128)} %copy.57) | copy-start | bytes 12582916
  632.2 3.1 copy-start.5
  636.4 7.5 collective-permute-start.2
  644.0 19.5 %collective-permute-start.3 = (bf16[2,8,48,512]{3,2,1,0:T(8,128)(2,1)S(1)}, bf16[2,8,48,512]{3,2,1,0:T(8,128)(2,1)S(1)}, u32[]{:S(2)}, u32[]{:S(2)}) collective-permute-start(bf16[2,8,48,512]{3,2,1,0:T(8,128)(2,1)S(1)} %fusion.29), channel_id=1, source_target_pairs={{120,0},{0,8},{8,16},{16,24},{24,32},{32,40},{40,48},{48,56},{56,6... | collective-permute-start | bytes 2359304 | tf_op jit(solution)/shard_map/ppermute | solution.py:14
  664.6 0.7 copy-start.11
  664.7 1.4 copy-start.3
  947.7 1.4 copy-start.4
  947.8 1.4 copy-start.12
Sparse Core Ops, SparseCore 0:
  9.1 302.2 all-gather.8
  313.1 301.0 all-gather.10
  615.8 298.9 all-gather.6
where the time goes:
time: 965 us; the launch traced here: 958 us
  blocking collectives  301 us (31%)
  local copies, waits for them, and re-layouts  279 us (29%)
  waiting for transfers between devices  270 us (28%)
  matrix products  67.7 us (7%)
  other arithmetic  19.8 us (2%)
  between operations  13.6 us (1%)
    all_gather x1, blocking collectives, body(): lax.all_gather(w_proj, ('row', 'col'), axis=0, tiled=True)  301 us
    all_gather x1, waiting for transfers between devices, body(): lax.all_gather(w_fc2, ('row', 'col'), axis=0, tiled=True)  247 us
    gather x2, local copies, waits for them, and re-layouts, position_bias(): return jnp.transpose(16.0 * jax.nn.sigmoid(table[index]), (2, 0, 1))  235 us
    dot_general x1, matrix products, finish_block(): mlp_out = jnp.dot(hidden, w_fc2, preferred_element_type=jnp.float32)  32.9 us
    ppermute x4, waiting for transfers between devices, from_behind(): return lax.ppermute(block, axis, route)  21.7 us
  transfers between devices with their start and end apart: 7, of which 3 were waited for; matrix products, arithmetic and copies ran while one was open for 34% of the time, Pallas kernels for 0%

commit v1 on v0

v1 whole, which is shorter than its diff:
```python
import math

import jax
import jax.numpy as jnp
from jax import lax
from jax.experimental import pallas as pl
from jax.experimental.pallas import tpu as pltpu
from jax.sharding import PartitionSpec as P

MESH = pl.DeviceIdType.MESH
BF = jnp.bfloat16
F32 = jnp.float32
LOG2E = math.log2(math.e)
ROUTES = ((1, 2, 0), (2, 0, 1), (0, 1, 2))


def iota(shape, dim):
    return lax.broadcasted_iota(jnp.int32, shape, dim)


def layer_norm(value, gain):
    mean = jnp.mean(value, -1, keepdims=True)
    centered = value - mean
    variance = jnp.mean(centered * centered, -1, keepdims=True)
    return centered * lax.rsqrt(variance + 1e-05) * gain


def own_block(w_ref, lo, lanes, tmp):
    for quarter in range(4):
        at = lo + quarter * lanes
        tmp[4 * quarter : 4 * quarter + 4, :lanes] = w_ref[:, at : at + lanes].astype(F32)
    return tmp[:, :lanes].astype(BF)


def kernel(
    tok_hbm, region_ref, wqkv_ref, wproj_ref, wfc1_ref, wfc2_ref,
    gain1_ref, gain2_ref, table_ref, index_ref, scale_ref,
    out_hbm,
    raw, T, X, A, R, O, GQ, GP, G1, G2, WQ, WP, W1, W2,
    QKV, M, bias, tab, RS, RT, LB, FQ, FK, tmp,
    raw_sem, out_sem, g_send, g_recv, d_send, d_recv, h_send, h_recv, r_send, r_recv,
):
    row, col = lax.axis_index("row"), lax.axis_index("col")
    core = lax.rem(row, 2)
    at = (row // 4, col // 2, lax.rem(row // 2, 2) * 2 + lax.rem(col, 2))

    def chip(x, y, z, c):
        return {"row": x * 4 + (z // 2) * 2 + c, "col": y * 2 + lax.rem(z, 2)}

    def near(dr, dc):
        return {"row": lax.rem(row + dr + 16, 16), "col": lax.rem(col + dc + 8, 8)}

    def along(axis, step):
        spot = list(at)
        spot[axis] = lax.rem(spot[axis] + step, 4)
        return chip(*spot, core)

    sibling = chip(*at, 1 - core)
    loads = [pltpu.make_async_copy(tok_hbm.at[i], raw.at[i], raw_sem.at[i]) for i in range(2)]
    for copy in loads:
        copy.start()

    peers = [along(axis, step) for axis in range(3) for step in (1, 2, 3)] + [sibling]
    peers += [near(-1, 0), near(1, 0), near(0, -1), near(0, 1), near(-1, -1), near(1, 1)]
    barrier = pltpu.get_barrier_semaphore()
    for peer in peers:
        pl.semaphore_signal(barrier, inc=1, device_id=peer, device_id_type=MESH)

    for flow in range(3):
        GQ[flow, core, at[0], at[1], at[2]] = own_block(wqkv_ref, 512 * flow, 128, tmp)
    GP[core, at[0], at[1], at[2]] = own_block(wproj_ref, 0, 128, tmp)
    G1[core, at[0], at[1], at[2]] = own_block(wfc1_ref, 0, 512, tmp)
    G2[core, at[0], at[1], at[2]] = wfc2_ref[...]
    RS[0] = jnp.zeros((16, 128), jnp.int32)
    RS[0, :, 0:48] = region_ref[...]

    pl.semaphore_wait(barrier, len(peers))

    sends = []

    def send(src, dst, s_sem, r_sem, device):
        copy = pltpu.make_async_remote_copy(
            src_ref=src, dst_ref=dst, send_sem=s_sem, recv_sem=r_sem,
            device_id=device, device_id_type=MESH,
        )
        copy.start()
        sends.append(copy)
        return copy

    batches = ([GQ.at[0], GQ.at[1], GQ.at[2]], [G1, G2, GP])

    def slab(batch, flow, known, axis=None, step=0):
        spot = list(at)
        if axis is not None:
            spot[axis] = lax.rem(spot[axis] + step, 4)
        pick = tuple(slice(None) if a in known else spot[a] for a in range(3))
        return batches[batch][flow].at[(core,) + pick]

    def gather_step(batch, step):
        copies = []
        for flow in range(3):
            route = ROUTES[flow]
            part = slab(batch, flow, route[:step])
            copies.append([
                send(part, part, g_send.at[batch, flow, step, t - 1], g_recv.at[batch, flow, step, t - 1],
                     along(route[step], t))
                for t in (1, 3, 2)
            ])
        return copies

    def across(batch, flow, piece):
        route = ROUTES[flow]
        part = slab(batch, flow, route[:2], route[2], piece)
        return send(part, part, d_send.at[batch, flow, piece], d_recv.at[batch, flow, piece], sibling)

    def await_all(copies):
        for group in copies:
            for copy in group:
                copy.wait_recv()

    def last_step(batch):
        final = gather_step(batch, 2)
        crossed = [across(batch, flow, 0) for flow in range(3)]
        return final, crossed

    def finish(batch, final, crossed):
        for order, piece in enumerate((3, 1, 2)):
            for flow in range(3):
                final[flow][order].wait_recv()
                crossed.append(across(batch, flow, piece))
        return crossed

    first = gather_step(0, 0)

    halo = [
        send(RS.at[0], RS.at[1], h_send.at[6], h_recv.at[6], near(1, 0)),
        send(RS.at[0], RS.at[2], h_send.at[7], h_recv.at[7], near(1, 1)),
    ]
    for image in range(2):
        loads[image].wait()
        for half in (image, 1 - image):
            rows = raw[image, 8 * half : 8 * half + 8].astype(F32)
            for group in range(6):
                part = rows[:, 8 * group : 8 * group + 8, :].reshape(64, 512).astype(BF)
                T[image, half, group] = part
                if image == 0 and half == 1 and group > 0:
                    X[0, 0, group - 1] = part
                if image == 1 and half == 0 and group < 5:
                    X[1, 1, group + 1] = part
        if image == 0:
            halo.append(send(T.at[0, 0, 1:6], X.at[0, 1, 0:5], h_send.at[0], h_recv.at[0], near(-1, 0)))
            halo.append(send(T.at[0, 0, 0], X.at[0, 1, 5], h_send.at[1], h_recv.at[1], near(-1, -1)))
            halo.append(send(T.at[0, 1, 0], X.at[0, 0, 5], h_send.at[2], h_recv.at[2], near(0, -1)))
        else:
            halo.append(send(T.at[1, 1, 0:5], X.at[1, 0, 1:6], h_send.at[3], h_recv.at[3], near(1, 0)))
            halo.append(send(T.at[1, 1, 5], X.at[1, 0, 0], h_send.at[4], h_recv.at[4], near(1, 1)))
            halo.append(send(T.at[1, 0, 5], X.at[1, 1, 0], h_send.at[5], h_recv.at[5], near(0, 1)))

    await_all(first)
    second = gather_step(0, 1)

    for chunk in range(8):
        base = 128 * chunk if chunk < 7 else 961 - 128
        tab[chunk] = (16.0 * LOG2E) * jax.nn.sigmoid(table_ref[base : base + 128, :].T)
    lane = iota((8, 128), 1)
    reorder = (lane // 8 % 8) * 16 + (lane // 64) * 8 + lane % 8

    def bias_rows(start, stop):
        def one(n, carry):
            source = (n // 16) * 128 + (n % 8) * 16 + (n // 8 % 2) * 8
            for half in range(2):
                index = index_ref[pl.ds(pl.multiple_of(source, 8), 8), 128 * half : 128 * half + 128]
                index = jnp.take_along_axis(index, reorder, axis=1, mode="promise_in_bounds")
                high = index // 128
                low = jnp.where(high == 7, index - (961 - 128), index % 128)
                for head in range(16):
                    found = jnp.zeros((8, 128), F32)
                    for chunk in range(8):
                        entry = jnp.broadcast_to(tab[chunk, head : head + 1, :], (8, 128))
                        value = jnp.take_along_axis(entry, low, axis=1, mode="promise_in_bounds")
                        found = jnp.where(high == chunk, value, found)
                    bias[head, pl.ds(pl.multiple_of(n * 8, 8), 8), 128 * half : 128 * half + 128] = found
            return carry

        lax.fori_loop(start, stop, one, 0)

    bias_rows(0, 16)
    await_all(second)
    final, crossed = last_step(0)
    other = gather_step(1, 0)
    bias_rows(16, 32)

    for copy in halo[:2]:
        copy.wait_recv()
    for place in range(3):
        RT[place] = RS[place].astype(F32).T

    crossed = finish(0, final, crossed)
    await_all(other)
    other = gather_step(1, 1)

    o, i = iota((256, 256), 0), iota((256, 256), 1)
    spot = (o // 8 % 4) * 64 + (o // 32 % 2) * 32 + (o // 4 % 2) * 16 + (o // 64) * 4 + o % 4
    permute = jnp.where(spot == i, 1.0, 0.0).astype(BF)
    squares = jnp.where(o // 32 == i // 32, 1.0, 0.0).astype(BF)

    def natural(source, dest, lanes):
        def one(n, carry):
            c, x = n // 4, n % 4
            found = jnp.dot(permute, source[c, x].reshape(256, lanes), preferred_element_type=F32).astype(BF)
            for quarter in range(4):
                for high in range(2):
                    base = 64 * quarter + 32 * high
                    to = pl.multiple_of(x * 128 + high * 64 + c * 32, 32)
                    dest[pl.ds(to, 32), lanes * quarter : lanes * quarter + lanes] = found[base : base + 32]
            return carry

        lax.fori_loop(0, 8, one, 0)

    for copy in crossed:
        copy.wait_recv()
    for flow in range(3):
        natural(GQ.at[flow], WQ.at[flow], 128)
    for copy in halo[2:]:
        copy.wait_recv()

    lane512 = iota((1, 512), 1)
    scale = jnp.zeros((1, 512), F32)
    for head in range(16):
        scale = jnp.where(lane512 // 32 == head, scale_ref[head] * LOG2E, scale)

    def project(w, carry):
        image, j = w // 3, w % 3
        x = X[image, :, pl.ds(2 * j, 2)].reshape(256, 512)
        for kind in range(3):
            value = jnp.dot(x, WQ[kind], preferred_element_type=F32)
            if kind < 2:
                square = (value * value).astype(BF)
                length = jnp.concatenate(
                    [jnp.dot(square[:, 256 * s : 256 * s + 256], squares, preferred_element_type=F32) for s in range(2)], 1)
                unit = lax.rsqrt(jnp.maximum(length, 1.0))
                value = value * (unit * scale if kind == 0 else unit)
            value = value.astype(BF)
            for block in range(4):
                QKV[w, kind, block] = value[:, 128 * block : 128 * block + 128]
        return carry

    lax.fori_loop(0, 6, project, 0)
    await_all(other)
    final, crossed = last_step(1)

    lane128 = iota((1, 128), 1)
    ones = jnp.ones((256, 128), BF)

    def attend(image, j):
        w = 3 * image + j
        place, start = (0, 16 * j) if image == 0 else ((2, 32) if j == 0 else (1, 16 * (j - 1)))
        for n in range(32):
            a, b = (n // 16) * 8 + n % 8, n // 8 % 2
            LB[8 * n : 8 * n + 8] = jnp.broadcast_to(RT[place, start + 8 * b : start + 8 * b + 8, a : a + 1], (8, 128))
        label = LB[...]
        for i in range(4):
            m = lane128 - 32 * ((i + 1) % 4)
            target = jnp.where((m >= 0) & (m < 6), m % 3, -1).astype(F32)
            hi, lo = 144.0, 100.0 * LOG2E - 144.0
            big = jnp.where(m < 3, hi, lo)
            rest = jnp.where(m == 6, -hi, jnp.where(m == 7, -lo, 0.0))
            unit = jnp.where((m == 6) | (m == 7), 1.0, 0.0)
            same = label == target
            FQ[i] = jnp.where(same, big, rest).astype(BF)
            FK[i] = jnp.where(same, 1.0, unit).astype(BF)

        def heads(block, carry):
            q, k = QKV[w, 0, block], QKV[w, 1, block]
            v = jnp.concatenate([QKV[w, 2, block], ones], 1)
            top = jnp.zeros((256, 128), F32)
            total = jnp.zeros((256, 128), F32)
            for i in range(4):
                here = lane128 // 32 == i
                keep = jnp.where(here, 1.0, 0.0).astype(BF)
                qh = q * keep + FQ[i]
                kh = k * keep + FK[i]
                score = lax.dot_general(qh, kh, (((1,), (1,)), ((), ())), preferred_element_type=F32)
                weight = jnp.exp2(score + bias[4 * block + i]).astype(BF)
                found = jnp.dot(weight, v, preferred_element_type=F32)
                top = jnp.where(here, found[:, :128], top)
                total = jnp.where(here, found[:, 128:], total)
            M[block] = (top / total).astype(BF)
            return carry

        lax.fori_loop(0, 4, heads, 0)
        mixed = jnp.concatenate([M[b] for b in range(4)], 1)
        done = jnp.dot(mixed, WP[...], preferred_element_type=F32).astype(BF).reshape(2, 2, 64, 512)
        for upper in range(2):
            for right in range(2):
                g = 2 * j + right
                if image == 0 and upper == 0 and g < 5:
                    R[0, 1, g + 1] = done[upper, right]
                elif image == 1 and upper == 1 and g > 0:
                    R[1, 0, g - 1] = done[upper, right]
                else:
                    A[image, upper, g] = done[upper, right]
        back = []
        for right in range(2):
            g = 2 * j + right
            s = 6 * image + g
            if image == 0:
                dst, to = (R.at[0, 0, g + 1], near(1, 0)) if g < 5 else (R.at[0, 0, 0], near(1, 1))
                back.append(send(A.at[0, 1, g], dst, r_send.at[s], r_recv.at[s], to))
                if g == 5:
                    back.append(send(A.at[0, 0, 5], R.at[0, 1, 0], r_send.at[12], r_recv.at[12], near(0, 1)))
            else:
                dst, to = (R.at[1, 1, g - 1], near(-1, 0)) if g > 0 else (R.at[1, 1, 5], near(-1, -1))
                back.append(send(A.at[1, 0, g], dst, r_send.at[s], r_recv.at[s], to))
                if g == 0:
                    back.append(send(A.at[1, 1, 0], R.at[1, 0, 5], r_send.at[13], r_recv.at[13], near(0, -1)))
        return back

    crossed = finish(1, final, crossed)
    for copy in crossed:
        copy.wait_recv()
    natural(GP, WP, 128)
    natural(G1, W1, 512)

    def second_rows(n, carry):
        c, x = n // 4, n % 4
        for high in range(2):
            for y in range(4):
                to = pl.multiple_of((x * 32 + high * 16 + c * 8 + y * 2) * 16, 32)
                W2[pl.ds(to, 32)] = G2[c, x, y, 2 * high : 2 * high + 2].reshape(32, 512)
        return carry

    lax.fori_loop(0, 8, second_rows, 0)

    back = {0: [], 1: []}
    for image, j in ((0, 2), (0, 0), (0, 1), (1, 0), (1, 1), (1, 2)):
        back[image] += attend(image, j)

    def mlp(image, half):
        after = T[image, half].reshape(384, 512).astype(F32)
        after = after + layer_norm(R[image, half].reshape(384, 512).astype(F32), gain1_ref[...])
        after = after.astype(BF)
        total = jnp.zeros((384, 512), F32)
        for part in range(4):
            hidden = jnp.dot(after, W1[:, 512 * part : 512 * part + 512], preferred_element_type=F32)
            hidden = 0.5 * hidden * (1.0 + lax.erf(hidden * math.sqrt(0.5)))
            total += jnp.dot(hidden.astype(BF), W2[512 * part : 512 * part + 512], preferred_element_type=F32)
        result = after.astype(F32) + layer_norm(total, gain2_ref[...])
        O[image, half] = result.astype(BF).reshape(6, 64, 512)
        copy = pltpu.make_async_copy(O.at[image, half], out_hbm.at[image, half], out_sem.at[image, half])
        copy.start()
        return copy

    outs = []
    for image in range(2):
        for copy in back[image]:
            copy.wait_recv()
        for half in (1 - image, image):
            outs.append(mlp(image, half))
    for copy in sends:
        copy.wait_send()
    for copy in outs:
        copy.wait()


def body(
    tokens, region, w_qkv, w_proj, w_fc1, w_fc2, gain_attn, gain_mlp, table, index, logit_scale
):
    vmem = pl.BlockSpec(memory_space=pltpu.VMEM)
    DMA = pltpu.SemaphoreType.DMA
    V = pltpu.VMEM
    tiles = (2, 2, 6, 64, 512)
    out = pl.pallas_call(
        kernel,
        out_shape=jax.ShapeDtypeStruct(tiles, BF),
        in_specs=[pl.BlockSpec(memory_space=pl.ANY)] + [vmem] * 9 + [pl.BlockSpec(memory_space=pltpu.SMEM)],
        out_specs=pl.BlockSpec(memory_space=pl.ANY),
        scratch_shapes=[
            V((2, 16, 48, 512), BF), V(tiles, BF), V(tiles, BF), V(tiles, BF), V(tiles, BF), V(tiles, BF),
            V((3, 2, 4, 4, 4, 16, 128), BF), V((2, 4, 4, 4, 16, 128), BF),
            V((2, 4, 4, 4, 16, 512), BF), V((2, 4, 4, 4, 16, 512), BF),
            V((3, 512, 512), BF), V((512, 512), BF), V((512, 2048), BF), V((2048, 512), BF),
            V((6, 3, 4, 256, 128), BF), V((4, 256, 128), BF), V((16, 256, 256), F32), V((8, 16, 128), F32),
            V((3, 16, 128), jnp.int32), V((3, 128, 16), F32), V((256, 128), F32),
            V((4, 256, 128), BF), V((4, 256, 128), BF), V((16, 512), F32),
            DMA((2,)), DMA((2, 2)), DMA((2, 3, 3, 3)), DMA((2, 3, 3, 3)), DMA((2, 3, 4)), DMA((2, 3, 4)),
            DMA((8,)), DMA((8,)), DMA((14,)), DMA((14,)),
        ],
        compiler_params=pltpu.CompilerParams(
            collective_id=0, has_side_effects=True, vmem_limit_bytes=60 * 1024 * 1024
        ),
    )(
        tokens, region, w_qkv, w_proj, w_fc1, w_fc2,
        gain_attn.reshape(1, 512), gain_mlp.reshape(1, 512), table, index, logit_scale,
    )
    out = out.reshape(2, 2, 6, 8, 8, 512).transpose(0, 1, 3, 2, 4, 5)
    return out.reshape(2, 16, 48, 512)


def solution(mesh):
    split = P(("row", "col"), None)
    return jax.shard_map(
        body,
        mesh=mesh,
        in_specs=(P(None, "row", "col", None), P("row", "col"), split, split, split, split, P(), P(), P(), P(), P()),
        out_specs=P(None, "row", "col", None),
        check_vma=False,
    )
```

time: 965 us -> 96.3 us (0.10)
  blocking collectives: 301 us -> 0 us
  local copies, waits for them, and re-layouts: 279 us -> 4.57 us
  waiting for transfers between devices: 270 us -> 0 us
  Pallas kernels: 0 us -> 91.5 us
  matrix products: 67.7 us -> 0 us
  other arithmetic: 19.8 us -> 0 us
  between operations: 13.6 us -> 0.01 us
    all_gather x1 -> x0, blocking collectives: 301 us -> none  [body(): lax.all_gather(w_proj, ('row', 'col'), axis=0, tiled=True)]
    all_gather x3 -> x0, waiting for transfers between devices: 247 us -> none  [the longest x1 247 us: body(): lax.all_gather(w_fc2, ('row', 'col'), axis=0, tiled=True)]
    gather x2 -> x0, local copies, waits for them, and re-layouts: 235 us -> none  [position_bias(): return jnp.transpose(16.0 * jax.nn.sigmoid(table[index]), (2, 0, 1))]
    pallas_call x0 -> x1, Pallas kernels: none -> 91.5 us  [body(): pl.pallas_call(kernel, out_shape=jax.ShapeDtypeStruct(tiles, BF), in_spec...]
    dot_general x5 -> x0, matrix products: 67.7 us -> none  [the longest x1 32.9 us: finish_block(): mlp_out = jnp.dot(hidden, w_fc2, preferred_element_type=jnp.float32)]
    ppermute x4 -> x0, waiting for transfers between devices: 21.7 us -> none  [from_behind(): return lax.ppermute(block, axis, route)]
    unnamed x33 -> x1, local copies, waits for them, and re-layouts: 16.1 us -> 1.82 us
    reshape x2 -> x0, local copies, waits for them, and re-layouts: 10.4 us -> none  [the longest x1 10.3 us: attention(): projected.reshape(num_windows, win_length, 3, HEADS, channels // HEADS)]
  transfers between devices with their start and end apart: 7 -> 0, of which waited for: 3 -> 0; matrix products, arithmetic and copies ran while one was open for 34% -> 0% of each run, Pallas kernels for 0% -> 0%
where the time goes in v1:
time: 96.3 us; the launch traced here: 96.1 us
  Pallas kernels  91.5 us (95%)
  local copies, waits for them, and re-layouts  4.57 us (5%)
    pallas_call x1, Pallas kernels, body(): pl.pallas_call(kernel, out_shape=jax.ShapeDtypeStruct(tiles, BF), in_spec...  91.5 us
    transpose x1, local copies, waits for them, and re-layouts, body(): out = out.reshape(2, 2, 6, 8, 8, 512).transpose(0, 1, 3, 2, 4, 5)  2.75 us

profile of v1, /device:TPU:1, one launch (start us, length us, event | category | flops | bytes accessed | tf_op | source)
XLA Modules:
  0.0 96.1 jit_solution(3698728502014439648)
XLA Ops:
  0.0 1.8 %copy.12.table_ref = f32[961,16]{1,0:T(8,128)} copy(f32[961,16]{0,1:T(8,128)} %param.19) | data formatting | bytes 123008 | tf_op args[8]
  1.8 91.5 %shard_map.109 = bf16[2,2,6,64,512]{4,3,2,1,0:T(8,128)(2,1)} custom-call(bf16[2,16,48,512]{3,2,1,0:T(8,128)(2,1)} %tok_hbm.1, s32[16,48]{1,0:T(8,128)} %region_ref.1, bf16[4,1536]{1,0:T(4,128)(2,1)} %wqkv_ref.1, bf16[4,512]{1,0:T(4,128)(2,1)} %wproj_ref.1, bf16[4,2048]{1,0:T(4,128)(2,1)} %wfc1_ref.1, bf16[16,512]{1,0:T(8,128)(2,1)} %wfc2_ref.1, ...), custom_call_target="tpu_custom_call" | custom-call | tf_op jit(solution)/shard_map/pallas_call | solution.py:373
  93.4 2.7 %copy.13 = bf16[2,2,8,6,8,512]{5,4,3,2,1,0:T(8,128)(2,1)} copy(bf16[2,2,8,6,8,512]{5,4,2,3,1,0:T(8,128)(2,1)} %bitcast.6) | data formatting | bytes 3145728 | tf_op jit(solution)/shard_map/transpose | solution.py:396

commit v2 on v1

--- a/solution.py
+++ b/solution.py
@@ -38,7 +38,7 @@
     out_hbm,
     raw, T, X, A, R, O, GQ, GP, G1, G2, WQ, WP, W1, W2,
     QKV, M, bias, tab, RS, RT, LB, FQ, FK, tmp,
-    raw_sem, out_sem, g_send, g_recv, d_send, d_recv, h_send, h_recv, r_send, r_recv,
+    raw_sem, out_sem, p_send, p_recv, g_send, g_recv, d_send, d_recv, h_send, h_recv, r_send, r_recv,
 ):
     row, col = lax.axis_index("row"), lax.axis_index("col")
     core = lax.rem(row, 2)
@@ -60,7 +60,19 @@
     for copy in loads:
         copy.start()
 
-    peers = [along(axis, step) for axis in range(3) for step in (1, 2, 3)] + [sibling]
+    def moved(steps):
+        return chip(*[lax.rem(at[a] + steps[a], 4) for a in range(3)], core)
+
+    def plane(route):
+        steps = []
+        for n in (1, 3, 4, 12, 2, 8, 5, 7, 13, 15, 6, 14, 9, 11, 10):
+            step = [0, 0, 0]
+            step[route[0]], step[route[1]] = n % 4, n // 4
+            steps.append(tuple(step))
+        return steps
+
+    steps = sorted({step for route in ROUTES for step in plane(route)})
+    peers = [moved(step) for step in steps] + [sibling]
     peers += [near(-1, 0), near(1, 0), near(0, -1), near(0, 1), near(-1, -1), near(1, 1)]
     barrier = pltpu.get_barrier_semaphore()
     for peer in peers:
@@ -96,41 +108,46 @@
         pick = tuple(slice(None) if a in known else spot[a] for a in range(3))
         return batches[batch][flow].at[(core,) + pick]
 
-    def gather_step(batch, step):
-        copies = []
-        for flow in range(3):
-            route = ROUTES[flow]
-            part = slab(batch, flow, route[:step])
-            copies.append([
-                send(part, part, g_send.at[batch, flow, step, t - 1], g_recv.at[batch, flow, step, t - 1],
-                     along(route[step], t))
-                for t in (1, 3, 2)
-            ])
+    def spread(batch):
+        copies = [[] for flow in range(3)]
+        for n in range(15):
+            for flow in range(3):
+                part = slab(batch, flow, ())
+                copies[flow].append(
+                    send(part, part, p_send.at[batch, flow, n], p_recv.at[batch, flow, n], moved(plane(ROUTES[flow])[n]))
+                )
         return copies
+
+    def lines(batch, flow):
+        route = ROUTES[flow]
+        part = slab(batch, flow, route[:2])
+        return [
+            send(part, part, g_send.at[batch, flow, t - 1], g_recv.at[batch, flow, t - 1], along(route[2], t))
+            for t in (1, 3, 2)
+        ]
 
     def across(batch, flow, piece):
         route = ROUTES[flow]
         part = slab(batch, flow, route[:2], route[2], piece)
         return send(part, part, d_send.at[batch, flow, piece], d_recv.at[batch, flow, piece], sibling)
 
-    def await_all(copies):
-        for group in copies:
-            for copy in group:
+    def last_step(batch, flows, planes):
+        final, crossed = {}, []
+        for flow in flows:
+            for copy in planes[flow]:
                 copy.wait_recv()
-
-    def last_step(batch):
-        final = gather_step(batch, 2)
-        crossed = [across(batch, flow, 0) for flow in range(3)]
+            final[flow] = lines(batch, flow)
+        for flow in flows:
+            crossed.append(across(batch, flow, 0))
         return final, crossed
 
-    def finish(batch, final, crossed):
-        for order, piece in enumerate((3, 1, 2)):
-            for flow in range(3):
+    def pass_on(batch, final, crossed, orders=(0, 1, 2)):
+        for order in orders:
+            for flow in final:
                 final[flow][order].wait_recv()
-                crossed.append(across(batch, flow, piece))
-        return crossed
-
-    first = gather_step(0, 0)
+                crossed.append(across(batch, flow, (3, 1, 2)[order]))
+
+    first = spread(0)
 
     halo = [
         send(RS.at[0], RS.at[1], h_send.at[6], h_recv.at[6], near(1, 0)),
@@ -156,82 +173,81 @@
             halo.append(send(T.at[1, 1, 5], X.at[1, 0, 0], h_send.at[4], h_recv.at[4], near(1, 1)))
             halo.append(send(T.at[1, 0, 5], X.at[1, 1, 0], h_send.at[5], h_recv.at[5], near(0, 1)))
 
-    await_all(first)
-    second = gather_step(0, 1)
-
-    for chunk in range(8):
-        base = 128 * chunk if chunk < 7 else 961 - 128
-        tab[chunk] = (16.0 * LOG2E) * jax.nn.sigmoid(table_ref[base : base + 128, :].T)
+
+    levels = jnp.round((2048.0 * 16.0 * LOG2E) * jax.nn.sigmoid(table_ref[...])).astype(jnp.int32)
+    pairs = levels[0:8] + (levels[8:16] - 32768) * 65536
+    for chunk in range(7):
+        tab[chunk] = pairs[:, 128 * chunk : 128 * chunk + 128]
+    tab[7, :, 0:65] = pairs[:, 896:961]
     lane = iota((8, 128), 1)
     reorder = (lane // 8 % 8) * 16 + (lane // 64) * 8 + lane % 8
 
     def bias_rows(start, stop):
         def one(n, carry):
             source = (n // 16) * 128 + (n % 8) * 16 + (n // 8 % 2) * 8
+            to = pl.ds(pl.multiple_of(n * 8, 8), 8)
             for half in range(2):
-                index = index_ref[pl.ds(pl.multiple_of(source, 8), 8), 128 * half : 128 * half + 128]
+                lanes = slice(128 * half, 128 * half + 128)
+                index = index_ref[pl.ds(pl.multiple_of(source, 8), 8), lanes]
                 index = jnp.take_along_axis(index, reorder, axis=1, mode="promise_in_bounds")
-                high = index // 128
-                low = jnp.where(high == 7, index - (961 - 128), index % 128)
-                for head in range(16):
-                    found = jnp.zeros((8, 128), F32)
+                high, low = index // 128, index % 128
+                for head in range(8):
+                    found = jnp.zeros((8, 128), jnp.int32)
                     for chunk in range(8):
                         entry = jnp.broadcast_to(tab[chunk, head : head + 1, :], (8, 128))
                         value = jnp.take_along_axis(entry, low, axis=1, mode="promise_in_bounds")
                         found = jnp.where(high == chunk, value, found)
-                    bias[head, pl.ds(pl.multiple_of(n * 8, 8), 8), 128 * half : 128 * half + 128] = found
+                    bias[head, to, lanes] = (found & 65535).astype(F32) * (1.0 / 2048.0)
+                    bias[head + 8, to, lanes] = (found >> 16).astype(F32) * (1.0 / 2048.0) + 16.0
             return carry
 
         lax.fori_loop(start, stop, one, 0)
 
-    bias_rows(0, 16)
-    await_all(second)
-    final, crossed = last_step(0)
-    other = gather_step(1, 0)
-    bias_rows(16, 32)
+    bias_rows(0, 6)
+    final, crossed = last_step(0, (0, 1, 2), first)
+    other = spread(1)
+    bias_rows(6, 24)
+    pass_on(0, final, crossed)
+    bias_rows(24, 32)
 
     for copy in halo[:2]:
         copy.wait_recv()
     for place in range(3):
         RT[place] = RS[place].astype(F32).T
 
-    crossed = finish(0, final, crossed)
-    await_all(other)
-    other = gather_step(1, 1)
-
     o, i = iota((256, 256), 0), iota((256, 256), 1)
     spot = (o // 8 % 4) * 64 + (o // 32 % 2) * 32 + (o // 4 % 2) * 16 + (o // 64) * 4 + o % 4
     permute = jnp.where(spot == i, 1.0, 0.0).astype(BF)
     squares = jnp.where(o // 32 == i // 32, 1.0, 0.0).astype(BF)
 
-    def natural(source, dest, lanes):
+    def natural(sources, dests, lanes, unroll):
         def one(n, carry):
             c, x = n // 4, n % 4
-            found = jnp.dot(permute, source[c, x].reshape(256, lanes), preferred_element_type=F32).astype(BF)
-            for quarter in range(4):
-                for high in range(2):
-                    base = 64 * quarter + 32 * high
-                    to = pl.multiple_of(x * 128 + high * 64 + c * 32, 32)
-                    dest[pl.ds(to, 32), lanes * quarter : lanes * quarter + lanes] = found[base : base + 32]
+            block = jnp.concatenate([source[c, x].reshape(256, lanes) for source in sources], 1)
+            found = jnp.dot(permute, block, preferred_element_type=F32).astype(BF)
+            for k, dest in enumerate(dests):
+                for quarter in range(4):
+                    for high in range(2):
+                        base = 64 * quarter + 32 * high
+                        to = pl.multiple_of(x * 128 + high * 64 + c * 32, 32)
+                        dest[pl.ds(to, 32), lanes * quarter : lanes * quarter + lanes] = found[
+                            base : base + 32, lanes * k : lanes * k + lanes
+                        ]
             return carry
 
-        lax.fori_loop(0, 8, one, 0)
+        lax.fori_loop(0, 8, one, 0, unroll=unroll)
 
     for copy in crossed:
         copy.wait_recv()
-    for flow in range(3):
-        natural(GQ.at[flow], WQ.at[flow], 128)
-    for copy in halo[2:]:
-        copy.wait_recv()
+    natural([GQ.at[flow] for flow in range(3)], [WQ.at[flow] for flow in range(3)], 128, True)
 
     lane512 = iota((1, 512), 1)
     scale = jnp.zeros((1, 512), F32)
     for head in range(16):
         scale = jnp.where(lane512 // 32 == head, scale_ref[head] * LOG2E, scale)
 
-    def project(w, carry):
-        image, j = w // 3, w % 3
-        x = X[image, :, pl.ds(2 * j, 2)].reshape(256, 512)
+    def project(image, upper):
+        x = X[image, upper].reshape(384, 512)
         for kind in range(3):
             value = jnp.dot(x, WQ[kind], preferred_element_type=F32)
             if kind < 2:
@@ -241,13 +257,21 @@
                 unit = lax.rsqrt(jnp.maximum(length, 1.0))
                 value = value * (unit * scale if kind == 0 else unit)
             value = value.astype(BF)
-            for block in range(4):
-                QKV[w, kind, block] = value[:, 128 * block : 128 * block + 128]
-        return carry
-
-    lax.fori_loop(0, 6, project, 0)
-    await_all(other)
-    final, crossed = last_step(1)
+            for j in range(3):
+                for block in range(4):
+                    QKV[3 * image + j, kind, block, 128 * upper : 128 * upper + 128] = value[
+                        128 * j : 128 * j + 128, 128 * block : 128 * block + 128
+                    ]
+
+    side = {0: halo[4], 1: halo[7]}
+    for image in range(2):
+        side[image].wait_recv()
+        project(image, image)
+    final, crossed = last_step(1, (2, 0, 1), other)
+    for image in range(2):
+        for copy in halo[2 + 3 * image : 4 + 3 * image]:
+            copy.wait_recv()
+        project(image, 1 - image)
 
     lane128 = iota((1, 128), 1)
     ones = jnp.ones((256, 128), BF)
@@ -316,12 +340,6 @@
                     back.append(send(A.at[1, 1, 0], R.at[1, 0, 5], r_send.at[13], r_recv.at[13], near(0, -1)))
         return back
 
-    crossed = finish(1, final, crossed)
-    for copy in crossed:
-        copy.wait_recv()
-    natural(GP, WP, 128)
-    natural(G1, W1, 512)
-
     def second_rows(n, carry):
         c, x = n // 4, n % 4
         for high in range(2):
@@ -330,11 +348,21 @@
                 W2[pl.ds(to, 32)] = G2[c, x, y, 2 * high : 2 * high + 2].reshape(32, 512)
         return carry
 
+    back = {0: [], 1: []}
+    ready = {2: final.pop(2)}
+    proj = [crossed.pop(0)]
+    pass_on(1, ready, proj)
+    for copy in proj:
+        copy.wait_recv()
+    natural([GP], [WP], 128, 2)
+    for n, (image, j) in enumerate(((0, 2), (0, 0), (0, 1), (1, 0), (1, 1), (1, 2))):
+        back[image] += attend(image, j)
+        if n in (0, 1, 2):
+            pass_on(1, final, crossed, (n,))
+    for copy in crossed:
+        copy.wait_recv()
+    natural([G1], [W1], 512, 2)
     lax.fori_loop(0, 8, second_rows, 0)
-
-    back = {0: [], 1: []}
-    for image, j in ((0, 2), (0, 0), (0, 1), (1, 0), (1, 1), (1, 2)):
-        back[image] += attend(image, j)
 
     def mlp(image, half):
         after = T[image, half].reshape(384, 512).astype(F32)
@@ -346,8 +374,9 @@
             hidden = 0.5 * hidden * (1.0 + lax.erf(hidden * math.sqrt(0.5)))
             total += jnp.dot(hidden.astype(BF), W2[512 * part : 512 * part + 512], preferred_element_type=F32)
         result = after.astype(F32) + layer_norm(total, gain2_ref[...])
-        O[image, half] = result.astype(BF).reshape(6, 64, 512)
-        copy = pltpu.make_async_copy(O.at[image, half], out_hbm.at[image, half], out_sem.at[image, half])
+        result = result.reshape(6, 8, 8, 512)
+        O[image, half] = jnp.concatenate([result[g] for g in range(6)], 1).astype(BF)
+        copy = pltpu.make_async_copy(O.at[image, half], out_hbm.at[image, 8 * half : 8 * half + 8], out_sem.at[image, half])
         copy.start()
         return copy
 
@@ -370,20 +399,20 @@
     DMA = pltpu.SemaphoreType.DMA
     V = pltpu.VMEM
     tiles = (2, 2, 6, 64, 512)
-    out = pl.pallas_call(
+    return pl.pallas_call(
         kernel,
-        out_shape=jax.ShapeDtypeStruct(tiles, BF),
+        out_shape=jax.ShapeDtypeStruct((2, 16, 48, 512), BF),
         in_specs=[pl.BlockSpec(memory_space=pl.ANY)] + [vmem] * 9 + [pl.BlockSpec(memory_space=pltpu.SMEM)],
         out_specs=pl.BlockSpec(memory_space=pl.ANY),
         scratch_shapes=[
-            V((2, 16, 48, 512), BF), V(tiles, BF), V(tiles, BF), V(tiles, BF), V(tiles, BF), V(tiles, BF),
+            V((2, 16, 48, 512), BF), V(tiles, BF), V(tiles, BF), V(tiles, BF), V(tiles, BF), V((2, 2, 8, 48, 512), BF),
             V((3, 2, 4, 4, 4, 16, 128), BF), V((2, 4, 4, 4, 16, 128), BF),
             V((2, 4, 4, 4, 16, 512), BF), V((2, 4, 4, 4, 16, 512), BF),
             V((3, 512, 512), BF), V((512, 512), BF), V((512, 2048), BF), V((2048, 512), BF),
-            V((6, 3, 4, 256, 128), BF), V((4, 256, 128), BF), V((16, 256, 256), F32), V((8, 16, 128), F32),
+            V((6, 3, 4, 256, 128), BF), V((4, 256, 128), BF), V((16, 256, 256), F32), V((8, 8, 128), jnp.int32),
             V((3, 16, 128), jnp.int32), V((3, 128, 16), F32), V((256, 128), F32),
             V((4, 256, 128), BF), V((4, 256, 128), BF), V((16, 512), F32),
-            DMA((2,)), DMA((2, 2)), DMA((2, 3, 3, 3)), DMA((2, 3, 3, 3)), DMA((2, 3, 4)), DMA((2, 3, 4)),
+            DMA((2,)), DMA((2, 2)), DMA((2, 3, 15)), DMA((2, 3, 15)), DMA((2, 3, 3)), DMA((2, 3, 3)), DMA((2, 3, 4)), DMA((2, 3, 4)),
             DMA((8,)), DMA((8,)), DMA((14,)), DMA((14,)),
         ],
         compiler_params=pltpu.CompilerParams(
@@ -391,10 +420,8 @@
         ),
     )(
         tokens, region, w_qkv, w_proj, w_fc1, w_fc2,
-        gain_attn.reshape(1, 512), gain_mlp.reshape(1, 512), table, index, logit_scale,
+        gain_attn.reshape(1, 512), gain_mlp.reshape(1, 512), table.T, index, logit_scale,
     )
-    out = out.reshape(2, 2, 6, 8, 8, 512).transpose(0, 1, 3, 2, 4, 5)
-    return out.reshape(2, 16, 48, 512)
 
 
 def solution(mesh):

time: 96.3 us -> 78.4 us (0.81)
  Pallas kernels: 91.5 us -> 75.6 us
  local copies, waits for them, and re-layouts: 4.57 us -> 2.66 us
    pallas_call x1, Pallas kernels: 91.5 us -> 75.6 us  [body(): pl.pallas_call(kernel, out_shape=jax.ShapeDtypeStruct((2, 16, 48, 512), B...]
    transpose x1 -> x0, local copies, waits for them, and re-layouts: 2.75 us -> none  [body(): out = out.reshape(2, 2, 6, 8, 8, 512).transpose(0, 1, 3, 2, 4, 5)]
where the time goes in v2:
time: 78.4 us; the launch traced here: 78.3 us
  Pallas kernels  75.6 us (96%)
  local copies, waits for them, and re-layouts  2.66 us (3%)
    pallas_call x1, Pallas kernels, body(): pl.pallas_call(kernel, out_shape=jax.ShapeDtypeStruct((2, 16, 48, 512), B...  75.6 us
    unnamed x1, local copies, waits for them, and re-layouts  2.66 us

profile of v2, /device:TPU:1, one launch (start us, length us, event | category | flops | bytes accessed | tf_op | source)
XLA Modules:
  0.0 78.3 jit_solution(18251298798865085294)
XLA Ops:
  0.0 75.6 %shard_map.109 = bf16[2,16,48,512]{3,2,1,0:T(8,128)(2,1)} custom-call(bf16[2,16,48,512]{3,2,1,0:T(8,128)(2,1)} %tok_hbm.1, s32[16,48]{1,0:T(8,128)} %region_ref.1, bf16[4,1536]{1,0:T(4,128)(2,1)} %wqkv_ref.1, bf16[4,512]{1,0:T(4,128)(2,1)} %wproj_ref.1, bf16[4,2048]{1,0:T(4,128)(2,1)} %wfc1_ref.1, bf16[16,512]{1,0:T(8,128)(2,1)} %wfc2_ref.1, ...), custom_call_target="tpu_custom_call" | custom-call | tf_op jit(solution)/shard_map/pallas_call | solution.py:402
  75.6 2.7 %copy.13 = bf16[2,16,48,512]{3,2,1,0:T(8,128)(2,1)} copy(bf16[2,16,48,512]{3,2,1,0:T(8,128)(2,1)} %shard_map.109) | data formatting | bytes 3145728

commit v3 on v2

--- a/solution.py
+++ b/solution.py
@@ -11,7 +11,7 @@
 BF = jnp.bfloat16
 F32 = jnp.float32
 LOG2E = math.log2(math.e)
-ROUTES = ((1, 2, 0), (2, 0, 1), (0, 1, 2))
+ROUTES = ((1, 0), (0, 1))
 
 
 def iota(shape, dim):
@@ -33,126 +33,58 @@
 
 
 def kernel(
-    tok_hbm, region_ref, wqkv_ref, wproj_ref, wfc1_ref, wfc2_ref,
-    gain1_ref, gain2_ref, table_ref, index_ref, scale_ref,
+    tok_hbm, region_hbm, wqkv_hbm, wproj_hbm, wfc1_hbm, wfc2_hbm,
+    gain1_hbm, gain2_hbm, table_hbm, index_hbm, scale_ref,
     out_hbm,
-    raw, T, X, A, R, O, GQ, GP, G1, G2, WQ, WP, W1, W2,
+    region_ref, wqkv_ref, wproj_ref, wfc1_ref, wfc2_ref, gain1_ref, gain2_ref, table_ref, index_ref,
+    raw, T, X, A, R, O, GQ, GP, GF, WQ, WP, W1, W2,
     QKV, M, bias, tab, RS, RT, LB, FQ, FK, tmp,
-    raw_sem, out_sem, p_send, p_recv, g_send, g_recv, d_send, d_recv, h_send, h_recv, r_send, r_recv,
+    raw_sem, in_sem, out_sem, z_send, z_recv, g_send, g_recv, d_send, d_recv, h_send, h_recv, r_send, r_recv,
 ):
     row, col = lax.axis_index("row"), lax.axis_index("col")
-    core = lax.rem(row, 2)
-    at = (row // 4, col // 2, lax.rem(row // 2, 2) * 2 + lax.rem(col, 2))
+    core = row & 1
+    at = (row >> 2, col >> 1, (row & 2) + (col & 1))
 
     def chip(x, y, z, c):
-        return {"row": x * 4 + (z // 2) * 2 + c, "col": y * 2 + lax.rem(z, 2)}
+        return {"row": x * 4 + (z & 2) + c, "col": y * 2 + (z & 1)}
 
     def near(dr, dc):
-        return {"row": lax.rem(row + dr + 16, 16), "col": lax.rem(col + dc + 8, 8)}
+        return {"row": (row + dr + 16) & 15, "col": (col + dc + 8) & 7}
 
     def along(axis, step):
         spot = list(at)
-        spot[axis] = lax.rem(spot[axis] + step, 4)
+        spot[axis] = (spot[axis] + step) & 3
         return chip(*spot, core)
 
     sibling = chip(*at, 1 - core)
-    loads = [pltpu.make_async_copy(tok_hbm.at[i], raw.at[i], raw_sem.at[i]) for i in range(2)]
-    for copy in loads:
-        copy.start()
-
-    def moved(steps):
-        return chip(*[lax.rem(at[a] + steps[a], 4) for a in range(3)], core)
-
-    def plane(route):
-        steps = []
-        for n in (1, 3, 4, 12, 2, 8, 5, 7, 13, 15, 6, 14, 9, 11, 10):
-            step = [0, 0, 0]
-            step[route[0]], step[route[1]] = n % 4, n // 4
-            steps.append(tuple(step))
-        return steps
-
-    steps = sorted({step for route in ROUTES for step in plane(route)})
-    peers = [moved(step) for step in steps] + [sibling]
+    peers = [along(axis, step) for axis in range(3) for step in (1, 2, 3)] + [sibling]
     peers += [near(-1, 0), near(1, 0), near(0, -1), near(0, 1), near(-1, -1), near(1, 1)]
     barrier = pltpu.get_barrier_semaphore()
     for peer in peers:
         pl.semaphore_signal(barrier, inc=1, device_id=peer, device_id_type=MESH)
 
+    inputs = [
+        pltpu.make_async_copy(source, dest, in_sem.at[n])
+        for n, (source, dest) in enumerate((
+            (wqkv_hbm, wqkv_ref), (wproj_hbm, wproj_ref), (region_hbm, region_ref), (wfc1_hbm, wfc1_ref),
+            (wfc2_hbm, wfc2_ref), (table_hbm, table_ref), (index_hbm, index_ref), (gain1_hbm, gain1_ref), (gain2_hbm, gain2_ref),
+        ))
+    ]
+    loads = [pltpu.make_async_copy(tok_hbm.at[i], raw.at[i], raw_sem.at[i]) for i in range(2)]
+    for copy in inputs + loads:
+        copy.start()
+    for copy in inputs:
+        copy.wait()
+
+    here = (core, at[0], at[1], at[2])
     for flow in range(3):
-        GQ[flow, core, at[0], at[1], at[2]] = own_block(wqkv_ref, 512 * flow, 128, tmp)
-    GP[core, at[0], at[1], at[2]] = own_block(wproj_ref, 0, 128, tmp)
-    G1[core, at[0], at[1], at[2]] = own_block(wfc1_ref, 0, 512, tmp)
-    G2[core, at[0], at[1], at[2]] = wfc2_ref[...]
+        GQ[here + (slice(None), slice(128 * flow, 128 * flow + 128))] = own_block(wqkv_ref, 512 * flow, 128, tmp)
+    GP[here] = own_block(wproj_ref, 0, 128, tmp)
+    GF[here + (slice(None), slice(0, 512))] = own_block(wfc1_ref, 0, 512, tmp)
+    GF[here + (slice(None), slice(512, 1024))] = wfc2_ref[...]
     RS[0] = jnp.zeros((16, 128), jnp.int32)
     RS[0, :, 0:48] = region_ref[...]
 
-    pl.semaphore_wait(barrier, len(peers))
-
-    sends = []
-
-    def send(src, dst, s_sem, r_sem, device):
-        copy = pltpu.make_async_remote_copy(
-            src_ref=src, dst_ref=dst, send_sem=s_sem, recv_sem=r_sem,
-            device_id=device, device_id_type=MESH,
-        )
-        copy.start()
-        sends.append(copy)
-        return copy
-
-    batches = ([GQ.at[0], GQ.at[1], GQ.at[2]], [G1, G2, GP])
-
-    def slab(batch, flow, known, axis=None, step=0):
-        spot = list(at)
-        if axis is not None:
-            spot[axis] = lax.rem(spot[axis] + step, 4)
-        pick = tuple(slice(None) if a in known else spot[a] for a in range(3))
-        return batches[batch][flow].at[(core,) + pick]
-
-    def spread(batch):
-        copies = [[] for flow in range(3)]
-        for n in range(15):
-            for flow in range(3):
-                part = slab(batch, flow, ())
-                copies[flow].append(
-                    send(part, part, p_send.at[batch, flow, n], p_recv.at[batch, flow, n], moved(plane(ROUTES[flow])[n]))
-                )
-        return copies
-
-    def lines(batch, flow):
-        route = ROUTES[flow]
-        part = slab(batch, flow, route[:2])
-        return [
-            send(part, part, g_send.at[batch, flow, t - 1], g_recv.at[batch, flow, t - 1], along(route[2], t))
-            for t in (1, 3, 2)
-        ]
-
-    def across(batch, flow, piece):
-        route = ROUTES[flow]
-        part = slab(batch, flow, route[:2], route[2], piece)
-        return send(part, part, d_send.at[batch, flow, piece], d_recv.at[batch, flow, piece], sibling)
-
-    def last_step(batch, flows, planes):
-        final, crossed = {}, []
-        for flow in flows:
-            for copy in planes[flow]:
-                copy.wait_recv()
-            final[flow] = lines(batch, flow)
-        for flow in flows:
-            crossed.append(across(batch, flow, 0))
-        return final, crossed
-
-    def pass_on(batch, final, crossed, orders=(0, 1, 2)):
-        for order in orders:
-            for flow in final:
-                final[flow][order].wait_recv()
-                crossed.append(across(batch, flow, (3, 1, 2)[order]))
-
-    first = spread(0)
-
-    halo = [
-        send(RS.at[0], RS.at[1], h_send.at[6], h_recv.at[6], near(1, 0)),
-        send(RS.at[0], RS.at[2], h_send.at[7], h_recv.at[7], near(1, 1)),
-    ]
     for image in range(2):
         loads[image].wait()
         for half in (image, 1 - image):
@@ -164,15 +96,76 @@
                     X[0, 0, group - 1] = part
                 if image == 1 and half == 0 and group < 5:
                     X[1, 1, group + 1] = part
-        if image == 0:
-            halo.append(send(T.at[0, 0, 1:6], X.at[0, 1, 0:5], h_send.at[0], h_recv.at[0], near(-1, 0)))
-            halo.append(send(T.at[0, 0, 0], X.at[0, 1, 5], h_send.at[1], h_recv.at[1], near(-1, -1)))
-            halo.append(send(T.at[0, 1, 0], X.at[0, 0, 5], h_send.at[2], h_recv.at[2], near(0, -1)))
-        else:
-            halo.append(send(T.at[1, 1, 0:5], X.at[1, 0, 1:6], h_send.at[3], h_recv.at[3], near(1, 0)))
-            halo.append(send(T.at[1, 1, 5], X.at[1, 0, 0], h_send.at[4], h_recv.at[4], near(1, 1)))
-            halo.append(send(T.at[1, 0, 5], X.at[1, 1, 0], h_send.at[5], h_recv.at[5], near(0, 1)))
-
+
+    pl.semaphore_wait(barrier, len(peers))
+
+    sends = []
+
+    def send(src, dst, s_sem, r_sem, device):
+        copy = pltpu.make_async_remote_copy(
+            src_ref=src, dst_ref=dst, send_sem=s_sem, recv_sem=r_sem,
+            device_id=device, device_id_type=MESH,
+        )
+        copy.start()
+        sends.append(copy)
+        return copy
+
+    batches = (GQ, GP, GF)
+
+    def step_z(batch):
+        part = batches[batch].at[here]
+        return [send(part, part, z_send.at[batch, t - 1], z_recv.at[batch, t - 1], along(2, t)) for t in (1, 3, 2)]
+
+    def slab(batch, flow, step, shift=0):
+        spot = list(at[:2])
+        axis = ROUTES[flow][step]
+        spot[axis] = (spot[axis] + shift) & 3
+        if step == 1:
+            spot[ROUTES[flow][0]] = slice(None)
+        return batches[batch].at[core, spot[0], spot[1], 2 * flow : 2 * flow + 2]
+
+    def step_xy(batch, step, before):
+        copies = {}
+        if step == 0:
+            for copy in before:
+                copy.wait_recv()
+        for flow in range(2):
+            if step == 1:
+                for copy in before[flow]:
+                    copy.wait_recv()
+            part = slab(batch, flow, step)
+            copies[flow] = [
+                send(part, part, g_send.at[batch, flow, step, t - 1], g_recv.at[batch, flow, step, t - 1],
+                     along(ROUTES[flow][step], t))
+                for t in (1, 3, 2)
+            ]
+        return copies
+
+    def across(batch, flow, piece):
+        part = slab(batch, flow, 1, piece)
+        return send(part, part, d_send.at[batch, flow, piece], d_recv.at[batch, flow, piece], sibling)
+
+    def pass_on(batch, final, orders=(0, 1, 2)):
+        crossed = []
+        for order in orders:
+            for flow in range(2):
+                final[flow][order].wait_recv()
+                crossed.append(across(batch, flow, (3, 1, 2)[order]))
+        return crossed
+
+    qkv = step_z(0)
+    halo = [
+        send(RS.at[0], RS.at[1], h_send.at[6], h_recv.at[6], near(1, 0)),
+        send(RS.at[0], RS.at[2], h_send.at[7], h_recv.at[7], near(1, 1)),
+        send(T.at[0, 0, 1:6], X.at[0, 1, 0:5], h_send.at[0], h_recv.at[0], near(-1, 0)),
+        send(T.at[0, 0, 0], X.at[0, 1, 5], h_send.at[1], h_recv.at[1], near(-1, -1)),
+        send(T.at[0, 1, 0], X.at[0, 0, 5], h_send.at[2], h_recv.at[2], near(0, -1)),
+        send(T.at[1, 1, 0:5], X.at[1, 0, 1:6], h_send.at[3], h_recv.at[3], near(1, 0)),
+        send(T.at[1, 1, 5], X.at[1, 0, 0], h_send.at[4], h_recv.at[4], near(1, 1)),
+        send(T.at[1, 0, 5], X.at[1, 1, 0], h_send.at[5], h_recv.at[5], near(0, 1)),
+    ]
+    proj = step_z(1)
+    fc = step_z(2)
 
     levels = jnp.round((2048.0 * 16.0 * LOG2E) * jax.nn.sigmoid(table_ref[...])).astype(jnp.int32)
     pairs = levels[0:8] + (levels[8:16] - 32768) * 65536
@@ -203,12 +196,13 @@
 
         lax.fori_loop(start, stop, one, 0)
 
-    bias_rows(0, 6)
-    final, crossed = last_step(0, (0, 1, 2), first)
-    other = spread(1)
-    bias_rows(6, 24)
-    pass_on(0, final, crossed)
-    bias_rows(24, 32)
+    bias_rows(0, 8)
+    qkv = step_xy(0, 0, qkv)
+    bias_rows(8, 20)
+    qkv = step_xy(0, 1, qkv)
+    crossed = [across(0, flow, 0) for flow in range(2)]
+    proj = step_xy(1, 0, proj)
+    bias_rows(20, 32)
 
     for copy in halo[:2]:
         copy.wait_recv()
@@ -220,10 +214,10 @@
     permute = jnp.where(spot == i, 1.0, 0.0).astype(BF)
     squares = jnp.where(o // 32 == i // 32, 1.0, 0.0).astype(BF)
 
-    def natural(sources, dests, lanes, unroll):
+    def natural(source, first, lanes, dests, unroll):
         def one(n, carry):
             c, x = n // 4, n % 4
-            block = jnp.concatenate([source[c, x].reshape(256, lanes) for source in sources], 1)
+            block = source[c, x, :, :, :, first : first + lanes * len(dests)].reshape(256, lanes * len(dests))
             found = jnp.dot(permute, block, preferred_element_type=F32).astype(BF)
             for k, dest in enumerate(dests):
                 for quarter in range(4):
@@ -237,9 +231,13 @@
 
         lax.fori_loop(0, 8, one, 0, unroll=unroll)
 
+    crossed += pass_on(0, qkv)
+    proj = step_xy(1, 1, proj)
+    crossed_proj = [across(1, flow, 0) for flow in range(2)]
+    fc = step_xy(2, 0, fc)
     for copy in crossed:
         copy.wait_recv()
-    natural([GQ.at[flow] for flow in range(3)], [WQ.at[flow] for flow in range(3)], 128, True)
+    natural(GQ, 0, 128, [WQ.at[flow] for flow in range(3)], True)
 
     lane512 = iota((1, 512), 1)
     scale = jnp.zeros((1, 512), F32)
@@ -267,11 +265,13 @@
     for image in range(2):
         side[image].wait_recv()
         project(image, image)
-    final, crossed = last_step(1, (2, 0, 1), other)
+    crossed_proj += pass_on(1, proj)
     for image in range(2):
         for copy in halo[2 + 3 * image : 4 + 3 * image]:
             copy.wait_recv()
         project(image, 1 - image)
+    fc = step_xy(2, 1, fc)
+    crossed = [across(2, flow, 0) for flow in range(2)]
 
     lane128 = iota((1, 128), 1)
     ones = jnp.ones((256, 128), BF)
@@ -294,7 +294,7 @@
             FQ[i] = jnp.where(same, big, rest).astype(BF)
             FK[i] = jnp.where(same, 1.0, unit).astype(BF)
 
-        def heads(block, carry):
+        for block in range(4):
             q, k = QKV[w, 0, block], QKV[w, 1, block]
             v = jnp.concatenate([QKV[w, 2, block], ones], 1)
             top = jnp.zeros((256, 128), F32)
@@ -310,9 +310,6 @@
                 top = jnp.where(here, found[:, :128], top)
                 total = jnp.where(here, found[:, 128:], total)
             M[block] = (top / total).astype(BF)
-            return carry
-
-        lax.fori_loop(0, 4, heads, 0)
         mixed = jnp.concatenate([M[b] for b in range(4)], 1)
         done = jnp.dot(mixed, WP[...], preferred_element_type=F32).astype(BF).reshape(2, 2, 64, 512)
         for upper in range(2):
@@ -345,23 +342,20 @@
         for high in range(2):
             for y in range(4):
                 to = pl.multiple_of((x * 32 + high * 16 + c * 8 + y * 2) * 16, 32)
-                W2[pl.ds(to, 32)] = G2[c, x, y, 2 * high : 2 * high + 2].reshape(32, 512)
+                W2[pl.ds(to, 32)] = GF[c, x, y, 2 * high : 2 * high + 2, :, 512:1024].reshape(32, 512)
         return carry
 
     back = {0: [], 1: []}
-    ready = {2: final.pop(2)}
-    proj = [crossed.pop(0)]
-    pass_on(1, ready, proj)
-    for copy in proj:
+    for copy in crossed_proj:
         copy.wait_recv()
-    natural([GP], [WP], 128, 2)
+    natural(GP, 0, 128, [WP], True)
     for n, (image, j) in enumerate(((0, 2), (0, 0), (0, 1), (1, 0), (1, 1), (1, 2))):
         back[image] += attend(image, j)
-        if n in (0, 1, 2):
-            pass_on(1, final, crossed, (n,))
+        if n >= 3:
+            crossed += pass_on(2, fc, (n - 3,))
     for copy in crossed:
         copy.wait_recv()
-    natural([G1], [W1], 512, 2)
+    natural(GF, 0, 512, [W1], 4)
     lax.fori_loop(0, 8, second_rows, 0)
 
     def mlp(image, half):
@@ -395,24 +389,24 @@
 def body(
     tokens, region, w_qkv, w_proj, w_fc1, w_fc2, gain_attn, gain_mlp, table, index, logit_scale
 ):
-    vmem = pl.BlockSpec(memory_space=pltpu.VMEM)
     DMA = pltpu.SemaphoreType.DMA
     V = pltpu.VMEM
     tiles = (2, 2, 6, 64, 512)
     return pl.pallas_call(
         kernel,
         out_shape=jax.ShapeDtypeStruct((2, 16, 48, 512), BF),
-        in_specs=[pl.BlockSpec(memory_space=pl.ANY)] + [vmem] * 9 + [pl.BlockSpec(memory_space=pltpu.SMEM)],
+        in_specs=[pl.BlockSpec(memory_space=pl.ANY)] * 10 + [pl.BlockSpec(memory_space=pltpu.SMEM)],
         out_specs=pl.BlockSpec(memory_space=pl.ANY),
         scratch_shapes=[
+            V((16, 48), jnp.int32), V((4, 1536), BF), V((4, 512), BF), V((4, 2048), BF), V((16, 512), BF),
+            V((1, 512), F32), V((1, 512), F32), V((16, 961), F32), V((256, 256), jnp.int32),
             V((2, 16, 48, 512), BF), V(tiles, BF), V(tiles, BF), V(tiles, BF), V(tiles, BF), V((2, 2, 8, 48, 512), BF),
-            V((3, 2, 4, 4, 4, 16, 128), BF), V((2, 4, 4, 4, 16, 128), BF),
-            V((2, 4, 4, 4, 16, 512), BF), V((2, 4, 4, 4, 16, 512), BF),
+            V((2, 4, 4, 4, 16, 384), BF), V((2, 4, 4, 4, 16, 128), BF), V((2, 4, 4, 4, 16, 1024), BF),
             V((3, 512, 512), BF), V((512, 512), BF), V((512, 2048), BF), V((2048, 512), BF),
             V((6, 3, 4, 256, 128), BF), V((4, 256, 128), BF), V((16, 256, 256), F32), V((8, 8, 128), jnp.int32),
             V((3, 16, 128), jnp.int32), V((3, 128, 16), F32), V((256, 128), F32),
             V((4, 256, 128), BF), V((4, 256, 128), BF), V((16, 512), F32),
-            DMA((2,)), DMA((2, 2)), DMA((2, 3, 15)), DMA((2, 3, 15)), DMA((2, 3, 3)), DMA((2, 3, 3)), DMA((2, 3, 4)), DMA((2, 3, 4)),
+            DMA((2,)), DMA((9,)), DMA((2, 2)), DMA((3, 3)), DMA((3, 3)), DMA((3, 2, 2, 3)), DMA((3, 2, 2, 3)), DMA((3, 2, 4)), DMA((3, 2, 4)),
             DMA((8,)), DMA((8,)), DMA((14,)), DMA((14,)),
         ],
         compiler_params=pltpu.CompilerParams(

time: 78.4 us -> 67.8 us (0.86); the launches traced: 78.3 us -> 66.8 us
  Pallas kernels: 75.6 us -> 64.1 us
    pallas_call x1, Pallas kernels: 75.6 us -> 64.1 us  [body(): pl.pallas_call(kernel, out_shape=jax.ShapeDtypeStruct((2, 16, 48, 512), B...]
where the time goes in v3:
time: 67.8 us; the launch traced here: 66.8 us
  Pallas kernels  64.1 us (95%)
  local copies, waits for them, and re-layouts  2.66 us (4%)
    pallas_call x1, Pallas kernels, body(): pl.pallas_call(kernel, out_shape=jax.ShapeDtypeStruct((2, 16, 48, 512), B...  64.1 us
    unnamed x1, local copies, waits for them, and re-layouts  2.66 us

profile of v3, /device:TPU:1, one launch (start us, length us, event | category | flops | bytes accessed | tf_op | source)
XLA Modules:
  0.0 66.8 jit_solution(7609804416555167629)
XLA Ops:
  0.0 64.1 %shard_map.109 = bf16[2,16,48,512]{3,2,1,0:T(8,128)(2,1)} custom-call(bf16[2,16,48,512]{3,2,1,0:T(8,128)(2,1)} %tok_hbm.1, s32[16,48]{1,0:T(8,128)} %region_hbm.1, bf16[4,1536]{1,0:T(4,128)(2,1)} %wqkv_hbm.1, bf16[4,512]{1,0:T(4,128)(2,1)} %wproj_hbm.1, bf16[4,2048]{1,0:T(4,128)(2,1)} %wfc1_hbm.1, bf16[16,512]{1,0:T(8,128)(2,1)} %wfc2_hbm.1, ...), custom_call_target="tpu_custom_call" | custom-call | tf_op jit(solution)/shard_map/pallas_call | solution.py:395
  64.1 2.7 %copy.13 = bf16[2,16,48,512]{3,2,1,0:T(8,128)(2,1)} copy(bf16[2,16,48,512]{3,2,1,0:T(8,128)(2,1)} %shard_map.109) | data formatting | bytes 3145728

commit v4 on v3

--- a/solution.py
+++ b/solution.py
@@ -231,10 +231,11 @@
 
         lax.fori_loop(0, 8, one, 0, unroll=unroll)
 
-    crossed += pass_on(0, qkv)
+    crossed += pass_on(0, qkv, (0,))
+    fc = step_xy(2, 0, fc)
+    crossed += pass_on(0, qkv, (1, 2))
     proj = step_xy(1, 1, proj)
     crossed_proj = [across(1, flow, 0) for flow in range(2)]
-    fc = step_xy(2, 0, fc)
     for copy in crossed:
         copy.wait_recv()
     natural(GQ, 0, 128, [WQ.at[flow] for flow in range(3)], True)
@@ -265,13 +266,13 @@
     for image in range(2):
         side[image].wait_recv()
         project(image, image)
+    fc = step_xy(2, 1, fc)
+    crossed = [across(2, flow, 0) for flow in range(2)]
     crossed_proj += pass_on(1, proj)
     for image in range(2):
         for copy in halo[2 + 3 * image : 4 + 3 * image]:
             copy.wait_recv()
         project(image, 1 - image)
-    fc = step_xy(2, 1, fc)
-    crossed = [across(2, flow, 0) for flow in range(2)]
 
     lane128 = iota((1, 128), 1)
     ones = jnp.ones((256, 128), BF)
@@ -329,12 +330,12 @@
                 dst, to = (R.at[0, 0, g + 1], near(1, 0)) if g < 5 else (R.at[0, 0, 0], near(1, 1))
                 back.append(send(A.at[0, 1, g], dst, r_send.at[s], r_recv.at[s], to))
                 if g == 5:
-                    back.append(send(A.at[0, 0, 5], R.at[0, 1, 0], r_send.at[12], r_recv.at[12], near(0, 1)))
+                    side_back.append(send(A.at[0, 0, 5], R.at[0, 1, 0], r_send.at[12], r_recv.at[12], near(0, 1)))
             else:
                 dst, to = (R.at[1, 1, g - 1], near(-1, 0)) if g > 0 else (R.at[1, 1, 5], near(-1, -1))
                 back.append(send(A.at[1, 0, g], dst, r_send.at[s], r_recv.at[s], to))
                 if g == 0:
-                    back.append(send(A.at[1, 1, 0], R.at[1, 0, 5], r_send.at[13], r_recv.at[13], near(0, -1)))
+                    side_back.append(send(A.at[1, 1, 0], R.at[1, 0, 5], r_send.at[13], r_recv.at[13], near(0, -1)))
         return back
 
     def second_rows(n, carry):
@@ -346,6 +347,7 @@
         return carry
 
     back = {0: [], 1: []}
+    side_back = []
     for copy in crossed_proj:
         copy.wait_recv()
     natural(GP, 0, 128, [WP], True)
@@ -362,11 +364,11 @@
         after = T[image, half].reshape(384, 512).astype(F32)
         after = after + layer_norm(R[image, half].reshape(384, 512).astype(F32), gain1_ref[...])
         after = after.astype(BF)
-        total = jnp.zeros((384, 512), F32)
+        units = []
         for part in range(4):
             hidden = jnp.dot(after, W1[:, 512 * part : 512 * part + 512], preferred_element_type=F32)
-            hidden = 0.5 * hidden * (1.0 + lax.erf(hidden * math.sqrt(0.5)))
-            total += jnp.dot(hidden.astype(BF), W2[512 * part : 512 * part + 512], preferred_element_type=F32)
+            units.append((0.5 * hidden * (1.0 + lax.erf(hidden * math.sqrt(0.5)))).astype(BF))
+        total = jnp.dot(jnp.concatenate(units, 1), W2[...], preferred_element_type=F32)
         result = after.astype(F32) + layer_norm(total, gain2_ref[...])
         result = result.reshape(6, 8, 8, 512)
         O[image, half] = jnp.concatenate([result[g] for g in range(6)], 1).astype(BF)
@@ -376,10 +378,11 @@
 
     outs = []
     for image in range(2):
+        side_back[image].wait_recv()
+        outs.append(mlp(image, 1 - image))
         for copy in back[image]:
             copy.wait_recv()
-        for half in (1 - image, image):
-            outs.append(mlp(image, half))
+        outs.append(mlp(image, image))
     for copy in sends:
         copy.wait_send()
     for copy in outs:

time: 67.8 us -> 65.4 us (0.965)
  the two profiles are of different devices: /device:TPU:1 before, /device:TPU:7 now
where the time goes in v4:
time: 65.4 us; the launch traced here: 65.2 us
  Pallas kernels  62.5 us (96%)
  local copies, waits for them, and re-layouts  2.66 us (4%)
    pallas_call x1, Pallas kernels, body(): pl.pallas_call(kernel, out_shape=jax.ShapeDtypeStruct((2, 16, 48, 512), B...  62.5 us
    unnamed x1, local copies, waits for them, and re-layouts  2.66 us

profile of v4, /device:TPU:7, one launch (start us, length us, event | category | flops | bytes accessed | tf_op | source)
XLA Modules:
  0.0 65.2 jit_solution(17994189101027112582)
XLA Ops:
  0.0 62.5 %shard_map.109 = bf16[2,16,48,512]{3,2,1,0:T(8,128)(2,1)} custom-call(bf16[2,16,48,512]{3,2,1,0:T(8,128)(2,1)} %tok_hbm.1, s32[16,48]{1,0:T(8,128)} %region_hbm.1, bf16[4,1536]{1,0:T(4,128)(2,1)} %wqkv_hbm.1, bf16[4,512]{1,0:T(4,128)(2,1)} %wproj_hbm.1, bf16[4,2048]{1,0:T(4,128)(2,1)} %wfc1_hbm.1, bf16[16,512]{1,0:T(8,128)(2,1)} %wfc2_hbm.1, ...), custom_call_target="tpu_custom_call" | custom-call | tf_op jit(solution)/shard_map/pallas_call | solution.py:398
  62.5 2.7 %copy.13 = bf16[2,16,48,512]{3,2,1,0:T(8,128)(2,1)} copy(bf16[2,16,48,512]{3,2,1,0:T(8,128)(2,1)} %shard_map.109) | data formatting | bytes 3145728

commit v5 on v4

--- a/solution.py
+++ b/solution.py
@@ -153,7 +153,7 @@
                 crossed.append(across(batch, flow, (3, 1, 2)[order]))
         return crossed
 
-    qkv = step_z(0)
+    qkv, proj, fc = step_z(0), step_z(1), step_z(2)
     halo = [
         send(RS.at[0], RS.at[1], h_send.at[6], h_recv.at[6], near(1, 0)),
         send(RS.at[0], RS.at[2], h_send.at[7], h_recv.at[7], near(1, 1)),
@@ -164,8 +164,6 @@
         send(T.at[1, 1, 5], X.at[1, 0, 0], h_send.at[4], h_recv.at[4], near(1, 1)),
         send(T.at[1, 0, 5], X.at[1, 1, 0], h_send.at[5], h_recv.at[5], near(0, 1)),
     ]
-    proj = step_z(1)
-    fc = step_z(2)
 
     levels = jnp.round((2048.0 * 16.0 * LOG2E) * jax.nn.sigmoid(table_ref[...])).astype(jnp.int32)
     pairs = levels[0:8] + (levels[8:16] - 32768) * 65536
@@ -198,10 +196,12 @@
 
     bias_rows(0, 8)
     qkv = step_xy(0, 0, qkv)
-    bias_rows(8, 20)
+    proj = step_xy(1, 0, proj)
+    bias_rows(8, 14)
+    fc = step_xy(2, 0, fc)
+    bias_rows(14, 20)
     qkv = step_xy(0, 1, qkv)
     crossed = [across(0, flow, 0) for flow in range(2)]
-    proj = step_xy(1, 0, proj)
     bias_rows(20, 32)
 
     for copy in halo[:2]:
@@ -232,9 +232,9 @@
         lax.fori_loop(0, 8, one, 0, unroll=unroll)
 
     crossed += pass_on(0, qkv, (0,))
-    fc = step_xy(2, 0, fc)
+    proj = step_xy(1, 1, proj)
+    fc = step_xy(2, 1, fc)
     crossed += pass_on(0, qkv, (1, 2))
-    proj = step_xy(1, 1, proj)
     crossed_proj = [across(1, flow, 0) for flow in range(2)]
     for copy in crossed:
         copy.wait_recv()
@@ -266,7 +266,6 @@
     for image in range(2):
         side[image].wait_recv()
         project(image, image)
-    fc = step_xy(2, 1, fc)
     crossed = [across(2, flow, 0) for flow in range(2)]
     crossed_proj += pass_on(1, proj)
     for image in range(2):
@@ -353,8 +352,8 @@
     natural(GP, 0, 128, [WP], True)
     for n, (image, j) in enumerate(((0, 2), (0, 0), (0, 1), (1, 0), (1, 1), (1, 2))):
         back[image] += attend(image, j)
-        if n >= 3:
-            crossed += pass_on(2, fc, (n - 3,))
+        if n in (2, 3, 4):
+            crossed += pass_on(2, fc, (n - 2,))
     for copy in crossed:
         copy.wait_recv()
     natural(GF, 0, 512, [W1], 4)

time: 65.4 us -> 62.4 us (0.954)
  the two profiles are of different devices: /device:TPU:7 before, /device:TPU:1 now
where the time goes in v5:
time: 62.4 us; the launch traced here: 62.3 us
  Pallas kernels  59.6 us (96%)
  local copies, waits for them, and re-layouts  2.66 us (4%)
    pallas_call x1, Pallas kernels, body(): pl.pallas_call(kernel, out_shape=jax.ShapeDtypeStruct((2, 16, 48, 512), B...  59.6 us
    unnamed x1, local copies, waits for them, and re-layouts  2.66 us

profile of v5, /device:TPU:1, one launch (start us, length us, event | category | flops | bytes accessed | tf_op | source)
XLA Modules:
  0.0 62.3 jit_solution(1377419997305371448)
XLA Ops:
  0.0 59.6 %shard_map.109 = bf16[2,16,48,512]{3,2,1,0:T(8,128)(2,1)} custom-call(bf16[2,16,48,512]{3,2,1,0:T(8,128)(2,1)} %tok_hbm.1, s32[16,48]{1,0:T(8,128)} %region_hbm.1, bf16[4,1536]{1,0:T(4,128)(2,1)} %wqkv_hbm.1, bf16[4,512]{1,0:T(4,128)(2,1)} %wproj_hbm.1, bf16[4,2048]{1,0:T(4,128)(2,1)} %wfc1_hbm.1, bf16[16,512]{1,0:T(8,128)(2,1)} %wfc2_hbm.1, ...), custom_call_target="tpu_custom_call" | custom-call | tf_op jit(solution)/shard_map/pallas_call | solution.py:397
  59.6 2.7 %copy.13 = bf16[2,16,48,512]{3,2,1,0:T(8,128)(2,1)} copy(bf16[2,16,48,512]{3,2,1,0:T(8,128)(2,1)} %shard_map.109) | data formatting | bytes 3145728

commit v6 on v5

--- a/solution.py
+++ b/solution.py
@@ -209,6 +209,29 @@
     for place in range(3):
         RT[place] = RS[place].astype(F32).T
 
+    lane128 = iota((1, 128), 1)
+
+    def mask_lanes(image, j):
+        w = 3 * image + j
+        place, start = (0, 16 * j) if image == 0 else ((2, 32) if j == 0 else (1, 16 * (j - 1)))
+        for n in range(32):
+            a, b = (n // 16) * 8 + n % 8, n // 8 % 2
+            LB[8 * n : 8 * n + 8] = jnp.broadcast_to(RT[place, start + 8 * b : start + 8 * b + 8, a : a + 1], (8, 128))
+        label = LB[...]
+        for i in range(4):
+            m = lane128 - 32 * ((i + 1) % 4)
+            target = jnp.where((m >= 0) & (m < 6), m % 3, -1).astype(F32)
+            hi, lo = 144.0, 100.0 * LOG2E - 144.0
+            big = jnp.where(m < 3, hi, lo)
+            rest = jnp.where(m == 6, -hi, jnp.where(m == 7, -lo, 0.0))
+            unit = jnp.where((m == 6) | (m == 7), 1.0, 0.0)
+            same = label == target
+            FQ[w, i] = jnp.where(same, big, rest).astype(BF)
+            FK[w, i] = jnp.where(same, 1.0, unit).astype(BF)
+
+    for w in range(6):
+        mask_lanes(w // 3, w % 3)
+
     o, i = iota((256, 256), 0), iota((256, 256), 1)
     spot = (o // 8 % 4) * 64 + (o // 32 % 2) * 32 + (o // 4 % 2) * 16 + (o // 64) * 4 + o % 4
     permute = jnp.where(spot == i, 1.0, 0.0).astype(BF)
@@ -273,27 +296,10 @@
             copy.wait_recv()
         project(image, 1 - image)
 
-    lane128 = iota((1, 128), 1)
     ones = jnp.ones((256, 128), BF)
 
     def attend(image, j):
         w = 3 * image + j
-        place, start = (0, 16 * j) if image == 0 else ((2, 32) if j == 0 else (1, 16 * (j - 1)))
-        for n in range(32):
-            a, b = (n // 16) * 8 + n % 8, n // 8 % 2
-            LB[8 * n : 8 * n + 8] = jnp.broadcast_to(RT[place, start + 8 * b : start + 8 * b + 8, a : a + 1], (8, 128))
-        label = LB[...]
-        for i in range(4):
-            m = lane128 - 32 * ((i + 1) % 4)
-            target = jnp.where((m >= 0) & (m < 6), m % 3, -1).astype(F32)
-            hi, lo = 144.0, 100.0 * LOG2E - 144.0
-            big = jnp.where(m < 3, hi, lo)
-            rest = jnp.where(m == 6, -hi, jnp.where(m == 7, -lo, 0.0))
-            unit = jnp.where((m == 6) | (m == 7), 1.0, 0.0)
-            same = label == target
-            FQ[i] = jnp.where(same, big, rest).astype(BF)
-            FK[i] = jnp.where(same, 1.0, unit).astype(BF)
-
         for block in range(4):
             q, k = QKV[w, 0, block], QKV[w, 1, block]
             v = jnp.concatenate([QKV[w, 2, block], ones], 1)
@@ -302,8 +308,8 @@
             for i in range(4):
                 here = lane128 // 32 == i
                 keep = jnp.where(here, 1.0, 0.0).astype(BF)
-                qh = q * keep + FQ[i]
-                kh = k * keep + FK[i]
+                qh = q * keep + FQ[w, i]
+                kh = k * keep + FK[w, i]
                 score = lax.dot_general(qh, kh, (((1,), (1,)), ((), ())), preferred_element_type=F32)
                 weight = jnp.exp2(score + bias[4 * block + i]).astype(BF)
                 found = jnp.dot(weight, v, preferred_element_type=F32)
@@ -356,8 +362,8 @@
             crossed += pass_on(2, fc, (n - 2,))
     for copy in crossed:
         copy.wait_recv()
-    natural(GF, 0, 512, [W1], 4)
-    lax.fori_loop(0, 8, second_rows, 0)
+    natural(GF, 0, 512, [W1], True)
+    lax.fori_loop(0, 8, second_rows, 0, unroll=2)
 
     def mlp(image, half):
         after = T[image, half].reshape(384, 512).astype(F32)
@@ -407,7 +413,7 @@
             V((3, 512, 512), BF), V((512, 512), BF), V((512, 2048), BF), V((2048, 512), BF),
             V((6, 3, 4, 256, 128), BF), V((4, 256, 128), BF), V((16, 256, 256), F32), V((8, 8, 128), jnp.int32),
             V((3, 16, 128), jnp.int32), V((3, 128, 16), F32), V((256, 128), F32),
-            V((4, 256, 128), BF), V((4, 256, 128), BF), V((16, 512), F32),
+            V((6, 4, 256, 128), BF), V((6, 4, 256, 128), BF), V((16, 512), F32),
             DMA((2,)), DMA((9,)), DMA((2, 2)), DMA((3, 3)), DMA((3, 3)), DMA((3, 2, 2, 3)), DMA((3, 2, 2, 3)), DMA((3, 2, 4)), DMA((3, 2, 4)),
             DMA((8,)), DMA((8,)), DMA((14,)), DMA((14,)),
         ],

time: 62.4 us -> 61.9 us (level)
  no operation moved by 1% of the time
where the time goes in v6:
time: 61.9 us; the launch traced here: 61.8 us
  Pallas kernels  59.1 us (95%)
  local copies, waits for them, and re-layouts  2.66 us (4%)
    pallas_call x1, Pallas kernels, body(): pl.pallas_call(kernel, out_shape=jax.ShapeDtypeStruct((2, 16, 48, 512), B...  59.1 us
    unnamed x1, local copies, waits for them, and re-layouts  2.66 us

profile of v6, /device:TPU:1, one launch (start us, length us, event | category | flops | bytes accessed | tf_op | source)
XLA Modules:
  0.0 61.8 jit_solution(4798311880175170606)
XLA Ops:
  0.0 59.1 %shard_map.109 = bf16[2,16,48,512]{3,2,1,0:T(8,128)(2,1)} custom-call(bf16[2,16,48,512]{3,2,1,0:T(8,128)(2,1)} %tok_hbm.1, s32[16,48]{1,0:T(8,128)} %region_hbm.1, bf16[4,1536]{1,0:T(4,128)(2,1)} %wqkv_hbm.1, bf16[4,512]{1,0:T(4,128)(2,1)} %wproj_hbm.1, bf16[4,2048]{1,0:T(4,128)(2,1)} %wfc1_hbm.1, bf16[16,512]{1,0:T(8,128)(2,1)} %wfc2_hbm.1, ...), custom_call_target="tpu_custom_call" | custom-call | tf_op jit(solution)/shard_map/pallas_call | solution.py:403
  59.1 2.7 %copy.13 = bf16[2,16,48,512]{3,2,1,0:T(8,128)(2,1)} copy(bf16[2,16,48,512]{3,2,1,0:T(8,128)(2,1)} %shard_map.109) | data formatting | bytes 3145728
